TPU v7x, 32 devices: a whole 2x2x4 slice. The times are simulated.
32 devices in a mesh: shots: 2 (over y), freq: 4 (over x, core), tile: 4 (over z).
Axes of the slice: x: 2, y: 2, z: 4, core: 2. Of those that a mesh axis runs over, the one named last changes fastest.
Arguments:
- velocity: float32 [4, 96, 1024], P(None, 'tile', 'freq'), may hold values from 1.5 to 4.5
- src_cell: int32 [8192], P('shots'), parts along dimension 0, may hold values from 0 to 98303
- src_wave: float32 [2, 4, 8192], P(None, 'freq', 'shots'), parts along dimension 2, may hold values from -24 to 24
- rec_cell: int32 [32768], P('shots'), parts along dimension 0, may hold values from 0 to 98303
- rec_data: float32 [2, 4, 32768], P(None, 'freq', 'shots'), parts along dimension 2, may hold values from -24 to 24
Outputs:
- final_fields: float32 [4, 4, 2, 96, 1024], P('shots', 'freq', None, 'tile'), parts along dimension 0
- migrated_image: float32 [8, 96, 1024], P('shots', 'tile', 'freq'), parts along dimension 0
There are 2 independent parts, one for each index of `shots`. A program takes and returns all parts, laid end to end along the dimension named above; an argument that names none is the same for every part. Nothing has to cross between parts.
Inputs may be any that keep to these rules, and one draw needn't show every extreme that they name: `src_cell`: each entry is a surface cell numbered row * 1024 + column; cells may repeat. `rec_cell`: each entry is a surface cell numbered row * 1024 + column; cells may repeat.
All inputs are finite; a program needn't handle non-finite values.
Results may differ from a plain program's by a relative error of at most 0.00002.
Values sent between devices are 32-bit elements; how exact they have to be, the bound alone decides.
A program may use at most 128 MiB of HBM per device.

v0:
```python
import functools
import math

import jax
import jax.numpy as jnp
from jax import lax
from jax.experimental import pallas as pl
from jax.experimental.pallas import tpu as pltpu
from jax.sharding import PartitionSpec as P

NY = 1024
STEPS = 4
PASSES = 5
LANES = 128
SUBLANES = 8

term_weights = (0.3, 0.25, -0.15, 0.12, -0.1, 0.08)
phase_unit = 0.25
slowest = 1.5

MESH = pl.DeviceIdType.MESH


def round_up(value, unit):
    return -(-value // unit) * unit


def series(angle, largest):
    square = angle * angle
    terms = 1
    while largest ** (2 * terms) / math.factorial(2 * terms) > 1e-9:
        terms += 1
    cos = sin = None
    for n in reversed(range(terms)):
        sign = -1.0 if n % 2 else 1.0
        even, odd = sign / math.factorial(2 * n), sign / math.factorial(2 * n + 1)
        cos = even if cos is None else cos * square + even
        sin = odd if sin is None else sin * square + odd
    return cos, sin * angle


def times(x, y):
    return x[0] * y[0] - x[1] * y[1], x[0] * y[1] + x[1] * y[0]


def double(x):
    twice = x[1] + x[1]
    return 1.0 - twice * x[1], twice * x[0]


def coefficients(kappa, largest):
    e15 = series(kappa * 0.15, largest * 0.15)
    e20 = series(kappa * 0.2, largest * 0.2)
    e30 = double(e15)
    e45 = times(e30, e15)
    e60 = double(e30)
    e80 = times(e60, e20)
    e100 = times(e80, e20)
    return [
        (w * c, w * s) for w, (c, s) in zip(term_weights, (e100, e80, e60, e45, e30, e20))
    ]


def kernel(
    freqs,
    tiles,
    velocity,
    src_cell,
    src_wave,
    rec_cell,
    rec_data,
    fields_out,
    image_out,
    speed,
    terms,
    sums,
    partial_image,
    image_in,
    speed_send,
    speed_recv,
    image_send,
    image_recv,
):
    f = lax.axis_index("freq")
    t = lax.axis_index("tile")
    rows = velocity.shape[1]
    own_cols = velocity.shape[2]
    blocks = NY // LANES
    halo = round_up(STEPS * PASSES, SUBLANES)
    window = rows + 2 * halo
    pad = SUBLANES
    has_above = t > 0
    has_below = t < tiles - 1

    groups = []
    for z in range(STEPS - 1):
        height = round_up(PASSES * (STEPS - 1 - z), SUBLANES)
        if groups and groups[-1][2] == height:
            groups[-1][1] = z + 1
        else:
            groups.append([z, z + 1, height])

    def other(step):
        return lax.rem(f + step, freqs)

    barrier = pltpu.get_barrier_semaphore()

    def greet(device):
        pl.semaphore_signal(barrier, inc=1, device_id=device, device_id_type=MESH)

    for step in range(1, freqs):
        greet({"freq": other(step)})

    @pl.when(has_above)
    def _():
        for step in range(freqs):
            greet({"freq": other(step), "tile": t - 1})

    @pl.when(has_below)
    def _():
        for step in range(freqs):
            greet({"freq": other(step), "tile": t + 1})

    neighbours = has_above.astype(jnp.int32) + has_below.astype(jnp.int32)
    pl.semaphore_wait(barrier, freqs - 1 + freqs * neighbours)

    def columns(owner):
        return pl.ds(pl.multiple_of(owner * own_cols, own_cols), own_cols)

    def level_copy(owner, target):
        return pltpu.make_async_remote_copy(
            src_ref=velocity,
            dst_ref=speed.at[:, pl.ds(halo, rows), columns(owner)],
            send_sem=speed_send.at[0, target, 0],
            recv_sem=speed_recv.at[0, owner, 0],
            device_id={"freq": target},
            device_id_type=MESH,
        )

    def down_copy(owner, target, g):
        low, high, height = groups[g]
        return pltpu.make_async_remote_copy(
            src_ref=velocity.at[pl.ds(low, high - low), pl.ds(rows - height, height)],
            dst_ref=speed.at[
                pl.ds(low, high - low), pl.ds(halo - height, height), columns(owner)
            ],
            send_sem=speed_send.at[1, target, g],
            recv_sem=speed_recv.at[1, owner, g],
            device_id={"freq": target, "tile": lax.rem(t + 1, tiles)},
            device_id_type=MESH,
        )

    def up_copy(owner, target, g):
        low, high, height = groups[g]
        return pltpu.make_async_remote_copy(
            src_ref=velocity.at[pl.ds(low, high - low), pl.ds(0, height)],
            dst_ref=speed.at[
                pl.ds(low, high - low), pl.ds(halo + rows, height), columns(owner)
            ],
            send_sem=speed_send.at[2, target, g],
            recv_sem=speed_recv.at[2, owner, g],
            device_id={"freq": target, "tile": lax.rem(t + tiles - 1, tiles)},
            device_id_type=MESH,
        )

    for step in range(1, freqs):
        level_copy(f, other(step)).start()

    @pl.when(has_below)
    def _():
        for g in range(len(groups)):
            for step in range(freqs):
                down_copy(f, other(step), g).start()

    @pl.when(has_above)
    def _():
        for g in range(len(groups)):
            for step in range(freqs):
                up_copy(f, other(step), g).start()

    speed[:, pl.ds(halo, rows), columns(f)] = velocity[...]

    @pl.when(jnp.logical_not(has_above))
    def _():
        speed[:, pl.ds(0, halo), :] = jnp.full((STEPS, halo, NY), 2.0, jnp.float32)

    @pl.when(jnp.logical_not(has_below))
    def _():
        speed[:, pl.ds(halo + rows, halo), :] = jnp.full((STEPS, halo, NY), 2.0, jnp.float32)

    for edge in (0, pad + window):
        terms[:, :, :, pl.ds(edge, pad), :] = jnp.zeros(
            (PASSES + 1, 4, blocks, pad, LANES), jnp.float32
        )

    first_row = t * rows - halo

    def inject(cells, data, field):
        count = cells.shape[1]
        chunk = math.gcd(count, 1024)
        sums[...] = jnp.zeros_like(sums)

        def add(i, carry):
            part = pl.ds(pl.multiple_of(i * chunk, chunk), chunk)
            cell = cells[:, part]
            row = (cell >> 10) - first_row
            col = cell & (NY - 1)
            inside = (row >= 0) & (row < window)
            place = jnp.where(inside, (col >> 7) * window + row, -1)
            lane = col & (LANES - 1)
            at_place = lax.broadcasted_iota(jnp.int32, (blocks * window, chunk), 0) == place
            at_lane = lax.broadcasted_iota(jnp.int32, (LANES, chunk), 0) == lane
            spread = []
            for c in range(2):
                value = data[c, :, part]
                head = value.astype(jnp.bfloat16).astype(jnp.float32)
                for piece in (head, value - head):
                    spread.append(jnp.where(at_lane, piece, 0.0).astype(jnp.bfloat16))
            one_hot = jnp.where(at_place, 1.0, 0.0).astype(jnp.bfloat16)
            sums[...] += lax.dot_general(
                one_hot,
                jnp.concatenate(spread, axis=0),
                (((1,), (1,)), ((), ())),
                preferred_element_type=jnp.float32,
            )
            return carry

        lax.fori_loop(0, count // chunk, add, 0)
        for c in range(2):
            for b in range(blocks):
                part = pl.ds(b * window, window)
                terms[0, 2 * field + c, b, pl.ds(pad, window), :] = (
                    sums[part, pl.ds(2 * c * LANES, LANES)]
                    + sums[part, pl.ds((2 * c + 1) * LANES, LANES)]
                )

    inject(src_cell, src_wave, 0)
    inject(rec_cell, rec_data, 1)

    for step in range(1, freqs):
        level_copy(other(step), other(step)).wait_recv()

    @pl.when(has_above)
    def _():
        for g in range(len(groups)):
            for owner in range(freqs):
                down_copy(owner, owner, g).wait_recv()

    @pl.when(has_below)
    def _():
        for g in range(len(groups)):
            for owner in range(freqs):
                up_copy(owner, owner, g).wait_recv()

    above_grid = jnp.where(has_above, 1.0, 0.0).astype(jnp.float32)
    below_grid = jnp.where(has_below, 1.0, 0.0).astype(jnp.float32)
    lane_index = lax.broadcasted_iota(jnp.int32, (SUBLANES, LANES), 1)
    at_first = lane_index == 0
    at_last = lane_index == LANES - 1
    number = (f + 1).astype(jnp.float32)
    largest = freqs * phase_unit / slowest

    def strips(margin):
        low = (halo - margin) // SUBLANES
        return range(low, round_up(halo + rows + margin, SUBLANES) // SUBLANES)

    def image_copy(z, owner, source):
        return pltpu.make_async_remote_copy(
            src_ref=partial_image.at[z, :, columns(owner)],
            dst_ref=image_in.at[z, source],
            send_sem=image_send.at[z, owner],
            recv_sem=image_recv.at[z, source],
            device_id={"freq": owner},
            device_id_type=MESH,
        )

    for z in range(STEPS):
        margin = PASSES * (STEPS - 1 - z)

        for k in range(1, PASSES + 1):

            def advance(plane, carry):
                for s in strips(margin + PASSES - k):
                    top = pad + s * SUBLANES
                    twice, tall = [], []
                    for b in range(blocks):
                        here = terms[k - 1, plane, b, pl.ds(top, SUBLANES), :]
                        over = terms[k - 1, plane, b, pl.ds(top - 1, SUBLANES), :]
                        under = terms[k - 1, plane, b, pl.ds(top + 1, SUBLANES), :]
                        twice.append(here + here)
                        tall.append(twice[b] + (over + under))
                    right = [pltpu.roll(v, 1, 1) for v in tall]
                    left = [pltpu.roll(v, LANES - 1, 1) for v in tall]
                    for b in range(blocks):
                        before = jnp.where(at_first, right[b - 1] if b else 0.0, right[b])
                        after = jnp.where(
                            at_last, left[b + 1] if b < blocks - 1 else 0.0, left[b]
                        )
                        wide = (tall[b] + tall[b]) + (before + after)
                        if k == 1:
                            new = 0.125 * wide - 0.5 * twice[b]
                        else:
                            new = (0.25 * wide - twice[b]) - terms[
                                k - 2, plane, b, pl.ds(top, SUBLANES), :
                            ]
                        if s * SUBLANES < halo:
                            new = new * above_grid
                        elif s * SUBLANES >= halo + rows:
                            new = new * below_grid
                        terms[k, plane, b, pl.ds(top, SUBLANES), :] = new
                return carry

            lax.fori_loop(0, 4, advance, 0)

        def combine(b, carry):
            lanes = pl.ds(pl.multiple_of(b * LANES, LANES), LANES)
            for s in strips(margin):
                top = pad + s * SUBLANES
                kappa = (number * phase_unit) / speed[z, pl.ds(s * SUBLANES, SUBLANES), lanes]
                total = [None] * 4
                for k, (real, imag) in enumerate(coefficients(kappa, largest)):
                    u = [terms[k, p, b, pl.ds(top, SUBLANES), :] for p in range(4)]
                    new = (
                        real * u[0] - imag * u[1],
                        real * u[1] + imag * u[0],
                        real * u[2] + imag * u[3],
                        real * u[3] - imag * u[2],
                    )
                    total = [n if o is None else o + n for o, n in zip(total, new)]
                own = s * SUBLANES - halo
                inside = 0 <= own < rows
                if z < STEPS - 1:
                    for p in range(4):
                        terms[0, p, b, pl.ds(top, SUBLANES), :] = total[p]
                else:
                    for p in range(4):
                        fields_out[p // 2, 0, p % 2, pl.ds(own, SUBLANES), lanes] = total[p]
                if inside:
                    partial_image[z, pl.ds(own, SUBLANES), lanes] = (
                        total[0] * total[2] + total[1] * total[3]
                    )
            return carry

        lax.fori_loop(0, blocks, combine, 0)
        for step in range(1, freqs):
            image_copy(z, other(step), f).start()

    for z in range(STEPS):
        whole = partial_image[z, :, columns(f)]
        for step in range(1, freqs):
            image_copy(z, f, other(step)).wait_recv()
            whole = whole + image_in[z, other(step)]
        image_out[z] = whole

    for z in range(STEPS):
        for step in range(1, freqs):
            image_copy(z, other(step), f).wait_send()
    for step in range(1, freqs):
        level_copy(f, other(step)).wait_send()

    @pl.when(has_below)
    def _():
        for g in range(len(groups)):
            for step in range(freqs):
                down_copy(f, other(step), g).wait_send()

    @pl.when(has_above)
    def _():
        for g in range(len(groups)):
            for step in range(freqs):
                up_copy(f, other(step), g).wait_send()


def body(freqs, tiles, velocity, src_cell, src_wave, rec_cell, rec_data):
    rows, own_cols = velocity.shape[1:]
    halo = round_up(STEPS * PASSES, SUBLANES)
    window = rows + 2 * halo
    blocks = NY // LANES
    assert src_wave.shape[1] == 1 and rows % SUBLANES == 0 and rows >= halo
    vmem = pl.BlockSpec(memory_space=pltpu.VMEM)
    return pl.pallas_call(
        functools.partial(kernel, freqs, tiles),
        out_shape=(
            jax.ShapeDtypeStruct((2, 1, 2, rows, NY), jnp.float32),
            jax.ShapeDtypeStruct((STEPS, rows, own_cols), jnp.float32),
        ),
        in_specs=[vmem] * 5,
        out_specs=(vmem, vmem),
        scratch_shapes=[
            pltpu.VMEM((STEPS, window, NY), jnp.float32),
            pltpu.VMEM((PASSES + 1, 4, blocks, window + 2 * SUBLANES, LANES), jnp.float32),
            pltpu.VMEM((blocks * window, 4 * LANES), jnp.float32),
            pltpu.VMEM((STEPS, rows, NY), jnp.float32),
            pltpu.VMEM((STEPS, freqs, rows, own_cols), jnp.float32),
            pltpu.SemaphoreType.DMA((3, freqs, STEPS)),
            pltpu.SemaphoreType.DMA((3, freqs, STEPS)),
            pltpu.SemaphoreType.DMA((STEPS, freqs)),
            pltpu.SemaphoreType.DMA((STEPS, freqs)),
        ],
        compiler_params=pltpu.CompilerParams(
            collective_id=0, has_side_effects=True, vmem_limit_bytes=40 * 1024 * 1024
        ),
    )(velocity, src_cell.reshape(1, -1), src_wave, rec_cell.reshape(1, -1), rec_data)


def solution(mesh):
    placed = (
        P(None, "tile", "freq"),
        P("shots"),
        P(None, "freq", "shots"),
        P("shots"),
        P(None, "freq", "shots"),
    )
    return jax.shard_map(
        functools.partial(body, mesh.shape["freq"], mesh.shape["tile"]),
        mesh=mesh,
        in_specs=placed,
        out_specs=(P("shots", "freq", None, "tile", None), P("shots", "tile", "freq")),
        check_vma=False,
    )
```

profile of v0, /device:TPU:0, one launch (start us, length us, event | category | flops | bytes accessed | tf_op | source)
XLA Modules:
  0.0 49.7 jit_solution(5183031136839574576)
XLA Ops:
  0.6 0.0 copy-start
  0.6 0.9 %copy-done = f32[2,1,16384]{2,1,0:T(1,128)S(1)} copy-done((f32[2,1,16384]{2,1,0:T(1,128)S(1)}, f32[2,1,16384]{2,1,0:T(1,128)}, u32[]{:S(2)}) %copy-start) | copy-done | bytes 131096
  1.5 0.0 copy-start.1
  1.5 0.9 %copy-done.1 = f32[4,24,256]{2,1,0:T(8,128)S(1)} copy-done((f32[4,24,256]{2,1,0:T(8,128)S(1)}, f32[4,24,256]{2,1,0:T(8,128)}, u32[]{:S(2)}) %copy-start.1) | copy-done | bytes 98328
  2.4 0.0 copy-start.2
  2.4 0.8 %copy-done.2 = s32[16384]{0:T(1024)S(1)} copy-done((s32[16384]{0:T(1024)S(1)}, s32[16384]{0:T(1024)}, u32[]{:S(2)}) %copy-start.2) | copy-done | bytes 65560
  3.3 0.0 copy-start.3
  3.3 0.8 %copy-done.3 = f32[2,1,4096]{2,1,0:T(1,128)S(1)} copy-done((f32[2,1,4096]{2,1,0:T(1,128)S(1)}, f32[2,1,4096]{2,1,0:T(1,128)}, u32[]{:S(2)}) %copy-start.3) | copy-done | bytes 32792
  4.0 0.0 copy-start.4
  4.0 0.7 %copy-done.4 = s32[4096]{0:T(1024)S(1)} copy-done((s32[4096]{0:T(1024)S(1)}, s32[4096]{0:T(1024)}, u32[]{:S(2)}) %copy-start.4) | copy-done | bytes 16408
  4.7 43.6 %shard_map.68 = (f32[2,1,2,24,1024]{4,3,2,1,0:T(8,128)S(1)}, f32[4,24,256]{2,1,0:T(8,128)S(1)}) custom-call(f32[4,24,256]{2,1,0:T(8,128)S(1)} %copy-done.1, s32[1,4096]{1,0:T(1,128)S(1)} %bitcast.3, f32[2,1,4096]{2,1,0:T(1,128)S(1)} %copy-done.3, s32[1,16384]{1,0:T(1,128)S(1)} %bitcast.2, f32[2,1,16384]{2,1,0:T(1,128)S(1)} %copy-done), custom_call_target="tpu_custom_call" | custom-call | tf_op jit(solution)/shard_map/pallas_call | solution.py:381
  48.3 0.7 %copy.9 = f32[2,1,2,24,1024]{4,3,2,1,0:T(8,128)} copy(f32[2,1,2,24,1024]{4,3,2,1,0:T(8,128)S(1)} %get-tuple-element.4) | data formatting | bytes 786432
  49.1 0.6 %copy.10 = f32[4,24,256]{2,1,0:T(8,128)} copy(f32[4,24,256]{2,1,0:T(8,128)S(1)} %get-tuple-element.5) | data formatting | bytes 196608
Async XLA Ops:
  0.6 0.9 %copy-start = (f32[2,1,16384]{2,1,0:T(1,128)S(1)}, f32[2,1,16384]{2,1,0:T(1,128)}, u32[]{:S(2)}) copy-start(f32[2,1,16384]{2,1,0:T(1,128)} %rec_data.1) | copy-start | bytes 393220
  1.5 0.9 %copy-start.1 = (f32[4,24,256]{2,1,0:T(8,128)S(1)}, f32[4,24,256]{2,1,0:T(8,128)}, u32[]{:S(2)}) copy-start(f32[4,24,256]{2,1,0:T(8,128)} %velocity.1) | copy-start | bytes 294916
  2.4 0.8 %copy-start.2 = (s32[16384]{0:T(1024)S(1)}, s32[16384]{0:T(1024)}, u32[]{:S(2)}) copy-start(s32[16384]{0:T(1024)} %param.8) | copy-start | bytes 196612
  3.3 0.8 %copy-start.3 = (f32[2,1,4096]{2,1,0:T(1,128)S(1)}, f32[2,1,4096]{2,1,0:T(1,128)}, u32[]{:S(2)}) copy-start(f32[2,1,4096]{2,1,0:T(1,128)} %src_wave.1) | copy-start | bytes 98308
  4.0 0.7 %copy-start.4 = (s32[4096]{0:T(1024)S(1)}, s32[4096]{0:T(1024)}, u32[]{:S(2)}) copy-start(s32[4096]{0:T(1024)} %param.6) | copy-start | bytes 49156
where the time goes:
time: 50.1 us; the launch traced here: 49.7 us
  Pallas kernels  43.6 us (87%)
  local copies, waits for them, and re-layouts  5.49 us (11%)
  between operations  0.65 us (1%)
    pallas_call x1, Pallas kernels, body(): pl.pallas_call(functools.partial(kernel, freqs, tiles), out_shape=(jax.Sh...  43.6 us
    unnamed x12, local copies, waits for them, and re-layouts  5.49 us

commit v1 on v0

--- a/solution.py
+++ b/solution.py
@@ -65,12 +65,16 @@
     freqs,
     tiles,
     velocity,
+    src_cell_in,
+    src_wave_in,
+    rec_cell_in,
+    rec_data_in,
+    fields_out,
+    image_out,
     src_cell,
     src_wave,
     rec_cell,
     rec_data,
-    fields_out,
-    image_out,
     speed,
     terms,
     sums,
@@ -80,13 +84,15 @@
     speed_recv,
     image_send,
     image_recv,
+    local,
 ):
     f = lax.axis_index("freq")
     t = lax.axis_index("tile")
     rows = velocity.shape[1]
     own_cols = velocity.shape[2]
     blocks = NY // LANES
-    halo = round_up(STEPS * PASSES, SUBLANES)
+    reach = STEPS * PASSES
+    halo = round_up(reach, SUBLANES)
     window = rows + 2 * halo
     pad = SUBLANES
     has_above = t > 0
@@ -103,6 +109,24 @@
     def other(step):
         return lax.rem(f + step, freqs)
 
+    def columns(owner):
+        return pl.ds(pl.multiple_of(owner * own_cols, own_cols), own_cols)
+
+    loads = [
+        pltpu.make_async_copy(source, target, local.at[i])
+        for i, (source, target) in enumerate(
+            (
+                (src_cell_in, src_cell),
+                (src_wave_in, src_wave),
+                (rec_cell_in, rec_cell),
+                (rec_data_in, rec_data),
+                (velocity, speed.at[:, pl.ds(halo, rows), columns(f)]),
+            )
+        )
+    ]
+    for load in loads:
+        load.start()
+
     barrier = pltpu.get_barrier_semaphore()
 
     def greet(device):
@@ -123,9 +147,6 @@
 
     neighbours = has_above.astype(jnp.int32) + has_below.astype(jnp.int32)
     pl.semaphore_wait(barrier, freqs - 1 + freqs * neighbours)
-
-    def columns(owner):
-        return pl.ds(pl.multiple_of(owner * own_cols, own_cols), own_cols)
 
     def level_copy(owner, target):
         return pltpu.make_async_remote_copy(
@@ -178,8 +199,6 @@
             for step in range(freqs):
                 up_copy(f, other(step), g).start()
 
-    speed[:, pl.ds(halo, rows), columns(f)] = velocity[...]
-
     @pl.when(jnp.logical_not(has_above))
     def _():
         speed[:, pl.ds(0, halo), :] = jnp.full((STEPS, halo, NY), 2.0, jnp.float32)
@@ -192,8 +211,15 @@
         terms[:, :, :, pl.ds(edge, pad), :] = jnp.zeros(
             (PASSES + 1, 4, blocks, pad, LANES), jnp.float32
         )
-
-    first_row = t * rows - halo
+    edge_rows = round_up(halo - reach, SUBLANES)
+    for edge in (pad, pad + window - edge_rows):
+        if edge_rows:
+            terms[0, :, :, pl.ds(edge, edge_rows), :] = jnp.zeros(
+                (4, blocks, edge_rows, LANES), jnp.float32
+            )
+
+    first_row = t * rows - reach
+    height = round_up(rows + 2 * reach, SUBLANES)
 
     def inject(cells, data, field):
         count = cells.shape[1]
@@ -205,18 +231,21 @@
             cell = cells[:, part]
             row = (cell >> 10) - first_row
             col = cell & (NY - 1)
-            inside = (row >= 0) & (row < window)
-            place = jnp.where(inside, (col >> 7) * window + row, -1)
+            inside = (row >= 0) & (row < height)
+            place = jnp.where(inside, (col >> 7) * height + row, -1)
             lane = col & (LANES - 1)
-            at_place = lax.broadcasted_iota(jnp.int32, (blocks * window, chunk), 0) == place
-            at_lane = lax.broadcasted_iota(jnp.int32, (LANES, chunk), 0) == lane
+            place, lane = place.astype(jnp.int16), lane.astype(jnp.int16)
+            at_place = lax.broadcasted_iota(jnp.int16, (blocks * height, chunk), 0) == place
+            at_lane = lax.broadcasted_iota(jnp.int16, (LANES, chunk), 0) == lane
+            one, zero = jnp.bfloat16(1.0), jnp.bfloat16(0.0)
             spread = []
             for c in range(2):
                 value = data[c, :, part]
-                head = value.astype(jnp.bfloat16).astype(jnp.float32)
-                for piece in (head, value - head):
-                    spread.append(jnp.where(at_lane, piece, 0.0).astype(jnp.bfloat16))
-            one_hot = jnp.where(at_place, 1.0, 0.0).astype(jnp.bfloat16)
+                head = value.astype(jnp.bfloat16)
+                rest = (value - head.astype(jnp.float32)).astype(jnp.bfloat16)
+                for piece in (head, rest):
+                    spread.append(jnp.where(at_lane, piece, zero))
+            one_hot = jnp.where(at_place, one, zero)
             sums[...] += lax.dot_general(
                 one_hot,
                 jnp.concatenate(spread, axis=0),
@@ -228,14 +257,19 @@
         lax.fori_loop(0, count // chunk, add, 0)
         for c in range(2):
             for b in range(blocks):
-                part = pl.ds(b * window, window)
-                terms[0, 2 * field + c, b, pl.ds(pad, window), :] = (
+                part = pl.ds(b * height, height)
+                terms[0, 2 * field + c, b, pl.ds(pad + halo - reach, height), :] = (
                     sums[part, pl.ds(2 * c * LANES, LANES)]
                     + sums[part, pl.ds((2 * c + 1) * LANES, LANES)]
                 )
 
+    loads[0].wait()
+    loads[1].wait()
     inject(src_cell, src_wave, 0)
+    loads[2].wait()
+    loads[3].wait()
     inject(rec_cell, rec_data, 1)
+    loads[4].wait()
 
     for step in range(1, freqs):
         level_copy(other(step), other(step)).wait_recv()
@@ -375,6 +409,8 @@
     rows, own_cols = velocity.shape[1:]
     halo = round_up(STEPS * PASSES, SUBLANES)
     window = rows + 2 * halo
+    height = round_up(rows + 2 * STEPS * PASSES, SUBLANES)
+    nsrc, nrec = src_cell.shape[0], rec_cell.shape[0]
     blocks = NY // LANES
     assert src_wave.shape[1] == 1 and rows % SUBLANES == 0 and rows >= halo
     vmem = pl.BlockSpec(memory_space=pltpu.VMEM)
@@ -384,21 +420,26 @@
             jax.ShapeDtypeStruct((2, 1, 2, rows, NY), jnp.float32),
             jax.ShapeDtypeStruct((STEPS, rows, own_cols), jnp.float32),
         ),
-        in_specs=[vmem] * 5,
+        in_specs=[pl.BlockSpec(memory_space=pltpu.HBM)] * 5,
         out_specs=(vmem, vmem),
         scratch_shapes=[
+            pltpu.VMEM((1, nsrc), jnp.int32),
+            pltpu.VMEM((2, 1, nsrc), jnp.float32),
+            pltpu.VMEM((1, nrec), jnp.int32),
+            pltpu.VMEM((2, 1, nrec), jnp.float32),
             pltpu.VMEM((STEPS, window, NY), jnp.float32),
             pltpu.VMEM((PASSES + 1, 4, blocks, window + 2 * SUBLANES, LANES), jnp.float32),
-            pltpu.VMEM((blocks * window, 4 * LANES), jnp.float32),
+            pltpu.VMEM((blocks * height, 4 * LANES), jnp.float32),
             pltpu.VMEM((STEPS, rows, NY), jnp.float32),
             pltpu.VMEM((STEPS, freqs, rows, own_cols), jnp.float32),
             pltpu.SemaphoreType.DMA((3, freqs, STEPS)),
             pltpu.SemaphoreType.DMA((3, freqs, STEPS)),
             pltpu.SemaphoreType.DMA((STEPS, freqs)),
             pltpu.SemaphoreType.DMA((STEPS, freqs)),
+            pltpu.SemaphoreType.DMA((5,)),
         ],
         compiler_params=pltpu.CompilerParams(
-            collective_id=0, has_side_effects=True, vmem_limit_bytes=40 * 1024 * 1024
+            collective_id=0, has_side_effects=True, vmem_limit_bytes=60 * 1024 * 1024
         ),
     )(velocity, src_cell.reshape(1, -1), src_wave, rec_cell.reshape(1, -1), rec_data)
 

time: 50.1 us -> 46.4 us (0.926)
  local copies, waits for them, and re-layouts: 5.49 us -> 2.45 us
    unnamed x12 -> x4, local copies, waits for them, and re-layouts: 5.49 us -> 2.45 us
where the time goes in v1:
time: 46.4 us; the launch traced here: 46.3 us
  Pallas kernels  43.2 us (93%)
  local copies, waits for them, and re-layouts  2.45 us (5%)
  between operations  0.65 us (1%)
    pallas_call x1, Pallas kernels, body(): pl.pallas_call(functools.partial(kernel, freqs, tiles), out_shape=(jax.Sh...  43.2 us
    unnamed x4, local copies, waits for them, and re-layouts  2.45 us

profile of v1, /device:TPU:0, one launch (start us, length us, event | category | flops | bytes accessed | tf_op | source)
XLA Modules:
  0.0 46.3 jit_solution(4010864602117039974)
XLA Ops:
  0.6 43.2 %shard_map.68 = (f32[2,1,2,24,1024]{4,3,2,1,0:T(8,128)}, f32[4,24,256]{2,1,0:T(8,128)}) custom-call(f32[4,24,256]{2,1,0:T(8,128)} %velocity.1, s32[1,4096]{1,0:T(1,128)} %bitcast.3, f32[2,1,4096]{2,1,0:T(1,128)} %src_wave_in.1, s32[1,16384]{1,0:T(1,128)} %bitcast.2, f32[2,1,16384]{2,1,0:T(1,128)} %rec_data_in.1), custom_call_target="tpu_custom_call" | custom-call | tf_op jit(solution)/shard_map/pallas_call | solution.py:417
  43.8 0.0 copy-start
  43.8 1.8 %copy.9 = f32[2,1,2,24,1024]{4,3,2,1,0:T(8,128)} copy(f32[2,1,2,24,1024]{4,3,2,1,0:T(8,128)} %get-tuple-element.4) | data formatting | bytes 786432
  45.6 0.0 copy-done
  45.6 0.6 %copy.10 = f32[4,24,256]{2,1,0:T(8,128)} copy(f32[4,24,256]{2,1,0:T(8,128)S(1)} %copy-done) | data formatting | bytes 196608
Async XLA Ops:
  43.8 1.8 %copy-start = (f32[4,24,256]{2,1,0:T(8,128)S(1)}, f32[4,24,256]{2,1,0:T(8,128)}, u32[]{:S(2)}) copy-start(f32[4,24,256]{2,1,0:T(8,128)} %get-tuple-element.5) | copy-start | bytes 294916

commit v2 on v1

--- a/solution.py
+++ b/solution.py
@@ -66,14 +66,18 @@
     tiles,
     velocity,
     src_cell_in,
+    src_fold_in,
     src_wave_in,
     rec_cell_in,
+    rec_fold_in,
     rec_data_in,
     fields_out,
     image_out,
     src_cell,
+    src_fold,
     src_wave,
     rec_cell,
+    rec_fold,
     rec_data,
     speed,
     terms,
@@ -117,8 +121,10 @@
         for i, (source, target) in enumerate(
             (
                 (src_cell_in, src_cell),
+                (src_fold_in, src_fold),
                 (src_wave_in, src_wave),
                 (rec_cell_in, rec_cell),
+                (rec_fold_in, rec_fold),
                 (rec_data_in, rec_data),
                 (velocity, speed.at[:, pl.ds(halo, rows), columns(f)]),
             )
@@ -220,10 +226,13 @@
 
     first_row = t * rows - reach
     height = round_up(rows + 2 * reach, SUBLANES)
-
-    def inject(cells, data, field):
+    wide = 2 * LANES
+    places = NY // wide * height
+
+    def inject(cells, fold, data, field):
         count = cells.shape[1]
-        chunk = math.gcd(count, 1024)
+        chunk = math.gcd(count, 2048)
+        folds = chunk // LANES
         sums[...] = jnp.zeros_like(sums)
 
         def add(i, carry):
@@ -232,24 +241,26 @@
             row = (cell >> 10) - first_row
             col = cell & (NY - 1)
             inside = (row >= 0) & (row < height)
-            place = jnp.where(inside, (col >> 7) * height + row, -1)
-            lane = col & (LANES - 1)
-            place, lane = place.astype(jnp.int16), lane.astype(jnp.int16)
-            at_place = lax.broadcasted_iota(jnp.int16, (blocks * height, chunk), 0) == place
-            at_lane = lax.broadcasted_iota(jnp.int16, (LANES, chunk), 0) == lane
-            one, zero = jnp.bfloat16(1.0), jnp.bfloat16(0.0)
+            place = jnp.where(inside, (col >> 8) * height + row, -1).astype(jnp.int16)
+            at_place = lax.broadcasted_iota(jnp.int16, (places, chunk), 0) == place
+            zero = jnp.bfloat16(0.0)
             spread = []
             for c in range(2):
                 value = data[c, :, part]
                 head = value.astype(jnp.bfloat16)
                 rest = (value - head.astype(jnp.float32)).astype(jnp.bfloat16)
                 for piece in (head, rest):
-                    spread.append(jnp.where(at_lane, piece, zero))
-            one_hot = jnp.where(at_place, one, zero)
-            sums[...] += lax.dot_general(
-                one_hot,
+                    spread.append(jnp.where(at_place, piece, zero))
+            lane = fold[pl.ds(pl.multiple_of(i * folds, folds), folds), :] & (wide - 1)
+            lane = lane.T
+            lanes = lax.broadcasted_iota(jnp.int32, (LANES, wide), 1)
+            one_hot = [
+                jnp.where(lanes == lane[:, q : q + 1], 1.0, 0.0).astype(jnp.bfloat16)
+                for q in range(folds)
+            ]
+            sums[...] += jnp.dot(
                 jnp.concatenate(spread, axis=0),
-                (((1,), (1,)), ((), ())),
+                jnp.concatenate(one_hot, axis=0),
                 preferred_element_type=jnp.float32,
             )
             return carry
@@ -257,19 +268,19 @@
         lax.fori_loop(0, count // chunk, add, 0)
         for c in range(2):
             for b in range(blocks):
-                part = pl.ds(b * height, height)
+                top = 2 * c * places + b // 2 * height
+                half = pl.ds(b % 2 * LANES, LANES)
                 terms[0, 2 * field + c, b, pl.ds(pad + halo - reach, height), :] = (
-                    sums[part, pl.ds(2 * c * LANES, LANES)]
-                    + sums[part, pl.ds((2 * c + 1) * LANES, LANES)]
+                    sums[pl.ds(top, height), half] + sums[pl.ds(top + places, height), half]
                 )
 
-    loads[0].wait()
-    loads[1].wait()
-    inject(src_cell, src_wave, 0)
-    loads[2].wait()
-    loads[3].wait()
-    inject(rec_cell, rec_data, 1)
-    loads[4].wait()
+    for load in loads[:3]:
+        load.wait()
+    inject(src_cell, src_fold, src_wave, 0)
+    for load in loads[3:6]:
+        load.wait()
+    inject(rec_cell, rec_fold, rec_data, 1)
+    loads[6].wait()
 
     for step in range(1, freqs):
         level_copy(other(step), other(step)).wait_recv()
@@ -313,14 +324,15 @@
 
         for k in range(1, PASSES + 1):
 
-            def advance(plane, carry):
-                for s in strips(margin + PASSES - k):
+            def advance(field, carry):
+                base = lax.div(field, 2)
+                for plane, s in [(2 * field + c, s) for c in range(2) for s in strips(margin + PASSES - k)]:
                     top = pad + s * SUBLANES
                     twice, tall = [], []
                     for b in range(blocks):
                         here = terms[k - 1, plane, b, pl.ds(top, SUBLANES), :]
-                        over = terms[k - 1, plane, b, pl.ds(top - 1, SUBLANES), :]
-                        under = terms[k - 1, plane, b, pl.ds(top + 1, SUBLANES), :]
+                        over = terms[k - 1, plane, b, pl.ds(base + (top - 1), SUBLANES), :]
+                        under = terms[k - 1, plane, b, pl.ds(base + (top + 1), SUBLANES), :]
                         twice.append(here + here)
                         tall.append(twice[b] + (over + under))
                     right = [pltpu.roll(v, 1, 1) for v in tall]
@@ -330,11 +342,11 @@
                         after = jnp.where(
                             at_last, left[b + 1] if b < blocks - 1 else 0.0, left[b]
                         )
-                        wide = (tall[b] + tall[b]) + (before + after)
+                        across = (tall[b] + tall[b]) + (before + after)
                         if k == 1:
-                            new = 0.125 * wide - 0.5 * twice[b]
+                            new = 0.125 * across - 0.5 * twice[b]
                         else:
-                            new = (0.25 * wide - twice[b]) - terms[
+                            new = (0.25 * across - twice[b]) - terms[
                                 k - 2, plane, b, pl.ds(top, SUBLANES), :
                             ]
                         if s * SUBLANES < halo:
@@ -344,7 +356,7 @@
                         terms[k, plane, b, pl.ds(top, SUBLANES), :] = new
                 return carry
 
-            lax.fori_loop(0, 4, advance, 0)
+            lax.fori_loop(0, 2, advance, 0)
 
         def combine(b, carry):
             lanes = pl.ds(pl.multiple_of(b * LANES, LANES), LANES)
@@ -420,28 +432,38 @@
             jax.ShapeDtypeStruct((2, 1, 2, rows, NY), jnp.float32),
             jax.ShapeDtypeStruct((STEPS, rows, own_cols), jnp.float32),
         ),
-        in_specs=[pl.BlockSpec(memory_space=pltpu.HBM)] * 5,
+        in_specs=[pl.BlockSpec(memory_space=pltpu.HBM)] * 7,
         out_specs=(vmem, vmem),
         scratch_shapes=[
             pltpu.VMEM((1, nsrc), jnp.int32),
+            pltpu.VMEM((nsrc // LANES, LANES), jnp.int32),
             pltpu.VMEM((2, 1, nsrc), jnp.float32),
             pltpu.VMEM((1, nrec), jnp.int32),
+            pltpu.VMEM((nrec // LANES, LANES), jnp.int32),
             pltpu.VMEM((2, 1, nrec), jnp.float32),
             pltpu.VMEM((STEPS, window, NY), jnp.float32),
             pltpu.VMEM((PASSES + 1, 4, blocks, window + 2 * SUBLANES, LANES), jnp.float32),
-            pltpu.VMEM((blocks * height, 4 * LANES), jnp.float32),
+            pltpu.VMEM((2 * blocks * height, 2 * LANES), jnp.float32),
             pltpu.VMEM((STEPS, rows, NY), jnp.float32),
             pltpu.VMEM((STEPS, freqs, rows, own_cols), jnp.float32),
             pltpu.SemaphoreType.DMA((3, freqs, STEPS)),
             pltpu.SemaphoreType.DMA((3, freqs, STEPS)),
             pltpu.SemaphoreType.DMA((STEPS, freqs)),
             pltpu.SemaphoreType.DMA((STEPS, freqs)),
-            pltpu.SemaphoreType.DMA((5,)),
+            pltpu.SemaphoreType.DMA((7,)),
         ],
         compiler_params=pltpu.CompilerParams(
             collective_id=0, has_side_effects=True, vmem_limit_bytes=60 * 1024 * 1024
         ),
-    )(velocity, src_cell.reshape(1, -1), src_wave, rec_cell.reshape(1, -1), rec_data)
+    )(
+        velocity,
+        src_cell.reshape(1, -1),
+        src_cell.reshape(-1, LANES),
+        src_wave,
+        rec_cell.reshape(1, -1),
+        rec_cell.reshape(-1, LANES),
+        rec_data,
+    )
 
 
 def solution(mesh):

time: 46.4 us -> 78.4 us (1.69)
  Pallas kernels: 43.2 us -> 75.1 us
    pallas_call x1, Pallas kernels: 43.2 us -> 75.1 us  [body(): pl.pallas_call(functools.partial(kernel, freqs, tiles), out_shape=(jax.Sh...]
where the time goes in v2:
time: 78.4 us; the launch traced here: 78.2 us
  Pallas kernels  75.1 us (96%)
  local copies, waits for them, and re-layouts  2.45 us (3%)
    pallas_call x1, Pallas kernels, body(): pl.pallas_call(functools.partial(kernel, freqs, tiles), out_shape=(jax.Sh...  75.1 us
    unnamed x4, local copies, waits for them, and re-layouts  2.45 us

profile of v2, /device:TPU:0, one launch (start us, length us, event | category | flops | bytes accessed | tf_op | source)
XLA Modules:
  0.0 78.2 jit_solution(10411448259580488743)
XLA Ops:
  0.6 75.1 %shard_map.68 = (f32[2,1,2,24,1024]{4,3,2,1,0:T(8,128)}, f32[4,24,256]{2,1,0:T(8,128)}) custom-call(f32[4,24,256]{2,1,0:T(8,128)} %velocity.1, s32[1,4096]{1,0:T(1,128)} %bitcast.6, s32[32,128]{1,0:T(8,128)} %bitcast.7, f32[2,1,4096]{2,1,0:T(1,128)} %src_wave_in.1, s32[1,16384]{1,0:T(1,128)} %bitcast.4, s32[128,128]{1,0:T(8,128)} %bitcast.5, ...), custom_call_target="tpu_custom_call" | custom-call | tf_op jit(solution)/shard_map/pallas_call | solution.py:429
  75.8 0.0 copy-start
  75.8 1.8 %copy.9 = f32[2,1,2,24,1024]{4,3,2,1,0:T(8,128)} copy(f32[2,1,2,24,1024]{4,3,2,1,0:T(8,128)} %get-tuple-element.4) | data formatting | bytes 786432
  77.6 0.0 copy-done
  77.6 0.6 copy.10
Async XLA Ops:
  75.8 1.8 %copy-start = (f32[4,24,256]{2,1,0:T(8,128)S(1)}, f32[4,24,256]{2,1,0:T(8,128)}, u32[]{:S(2)}) copy-start(f32[4,24,256]{2,1,0:T(8,128)} %get-tuple-element.5) | copy-start | bytes 294916

commit v3 on v1

--- a/solution.py
+++ b/solution.py
@@ -76,6 +76,9 @@
     rec_cell,
     rec_data,
     speed,
+    order,
+    speed_inside,
+    image_inside,
     terms,
     sums,
     partial_image,
@@ -127,6 +130,24 @@
     for load in loads:
         load.start()
 
+    for b in range(blocks):
+        column = lax.broadcasted_iota(jnp.int32, (NY, LANES), 0)
+        inner = lax.broadcasted_iota(jnp.int32, (NY, LANES), 1) * blocks + b
+        order[:, pl.ds(b * LANES, LANES)] = jnp.where(column == inner, 1.0, 0.0).astype(
+            jnp.bfloat16
+        )
+
+    def reordered(values, side):
+        head = values.astype(jnp.bfloat16)
+        rest = (values - head.astype(jnp.float32)).astype(jnp.bfloat16)
+        both = lax.dot_general(
+            jnp.concatenate([head, rest], axis=0),
+            order[...],
+            (((1,), (side,)), ((), ())),
+            preferred_element_type=jnp.float32,
+        )
+        return both[: values.shape[0]] + both[values.shape[0] :]
+
     barrier = pltpu.get_barrier_semaphore()
 
     def greet(device):
@@ -232,8 +253,8 @@
             row = (cell >> 10) - first_row
             col = cell & (NY - 1)
             inside = (row >= 0) & (row < height)
-            place = jnp.where(inside, (col >> 7) * height + row, -1)
-            lane = col & (LANES - 1)
+            place = jnp.where(inside, (col & (blocks - 1)) * height + row, -1)
+            lane = col >> (blocks.bit_length() - 1)
             place, lane = place.astype(jnp.int16), lane.astype(jnp.int16)
             at_place = lax.broadcasted_iota(jnp.int16, (blocks * height, chunk), 0) == place
             at_lane = lax.broadcasted_iota(jnp.int16, (LANES, chunk), 0) == lane
@@ -308,6 +329,42 @@
             device_id_type=MESH,
         )
 
+    spans = [strips(PASSES * (STEPS - 1 - z)) for z in range(STEPS)]
+    inner_speed = reordered(
+        jnp.concatenate(
+            [
+                speed[z, pl.ds(span[0] * SUBLANES, len(span) * SUBLANES), :]
+                for z, span in enumerate(spans)
+            ],
+            axis=0,
+        ),
+        0,
+    )
+    top = 0
+    for z, span in enumerate(spans):
+        extent = len(span) * SUBLANES
+        for b in range(blocks):
+            speed_inside[z, b, pl.ds(span[0] * SUBLANES, extent), :] = inner_speed[
+                top : top + extent, b * LANES : (b + 1) * LANES
+            ]
+        top += extent
+
+    def finish_images(low, high):
+        outer = reordered(
+            jnp.concatenate(
+                [
+                    jnp.concatenate([image_inside[z, b] for b in range(blocks)], axis=1)
+                    for z in range(low, high)
+                ],
+                axis=0,
+            ),
+            1,
+        )
+        for z in range(low, high):
+            partial_image[z] = outer[(z - low) * rows : (z - low + 1) * rows]
+            for step in range(1, freqs):
+                image_copy(z, other(step), f).start()
+
     for z in range(STEPS):
         margin = PASSES * (STEPS - 1 - z)
 
@@ -323,13 +380,9 @@
                         under = terms[k - 1, plane, b, pl.ds(top + 1, SUBLANES), :]
                         twice.append(here + here)
                         tall.append(twice[b] + (over + under))
-                    right = [pltpu.roll(v, 1, 1) for v in tall]
-                    left = [pltpu.roll(v, LANES - 1, 1) for v in tall]
                     for b in range(blocks):
-                        before = jnp.where(at_first, right[b - 1] if b else 0.0, right[b])
-                        after = jnp.where(
-                            at_last, left[b + 1] if b < blocks - 1 else 0.0, left[b]
-                        )
+                        before = tall[b - 1] if b else jnp.where(at_first, 0.0, pltpu.roll(tall[blocks - 1], 1, 1))
+                        after = tall[b + 1] if b < blocks - 1 else jnp.where(at_last, 0.0, pltpu.roll(tall[0], LANES - 1, 1))
                         wide = (tall[b] + tall[b]) + (before + after)
                         if k == 1:
                             new = 0.125 * wide - 0.5 * twice[b]
@@ -347,10 +400,9 @@
             lax.fori_loop(0, 4, advance, 0)
 
         def combine(b, carry):
-            lanes = pl.ds(pl.multiple_of(b * LANES, LANES), LANES)
             for s in strips(margin):
                 top = pad + s * SUBLANES
-                kappa = (number * phase_unit) / speed[z, pl.ds(s * SUBLANES, SUBLANES), lanes]
+                kappa = (number * phase_unit) / speed_inside[z, b, pl.ds(s * SUBLANES, SUBLANES), :]
                 total = [None] * 4
                 for k, (real, imag) in enumerate(coefficients(kappa, largest)):
                     u = [terms[k, p, b, pl.ds(top, SUBLANES), :] for p in range(4)]
@@ -363,21 +415,33 @@
                     total = [n if o is None else o + n for o, n in zip(total, new)]
                 own = s * SUBLANES - halo
                 inside = 0 <= own < rows
-                if z < STEPS - 1:
-                    for p in range(4):
-                        terms[0, p, b, pl.ds(top, SUBLANES), :] = total[p]
-                else:
-                    for p in range(4):
-                        fields_out[p // 2, 0, p % 2, pl.ds(own, SUBLANES), lanes] = total[p]
+                for p in range(4):
+                    terms[0, p, b, pl.ds(top, SUBLANES), :] = total[p]
                 if inside:
-                    partial_image[z, pl.ds(own, SUBLANES), lanes] = (
+                    image_inside[z, b, pl.ds(own, SUBLANES), :] = (
                         total[0] * total[2] + total[1] * total[3]
                     )
             return carry
 
         lax.fori_loop(0, blocks, combine, 0)
-        for step in range(1, freqs):
-            image_copy(z, other(step), f).start()
+        if z == STEPS - 2:
+            finish_images(0, STEPS - 1)
+        elif z == STEPS - 1:
+            finish_images(STEPS - 1, STEPS)
+
+    own_rows = pl.ds(pad + halo, rows)
+    outer_fields = reordered(
+        jnp.concatenate(
+            [
+                jnp.concatenate([terms[0, p, b, own_rows, :] for b in range(blocks)], axis=1)
+                for p in range(4)
+            ],
+            axis=0,
+        ),
+        1,
+    )
+    for p in range(4):
+        fields_out[p // 2, 0, p % 2] = outer_fields[p * rows : (p + 1) * rows]
 
     for z in range(STEPS):
         whole = partial_image[z, :, columns(f)]
@@ -428,6 +492,9 @@
             pltpu.VMEM((1, nrec), jnp.int32),
             pltpu.VMEM((2, 1, nrec), jnp.float32),
             pltpu.VMEM((STEPS, window, NY), jnp.float32),
+            pltpu.VMEM((NY, NY), jnp.bfloat16),
+            pltpu.VMEM((STEPS, blocks, window, LANES), jnp.float32),
+            pltpu.VMEM((STEPS, blocks, rows, LANES), jnp.float32),
             pltpu.VMEM((PASSES + 1, 4, blocks, window + 2 * SUBLANES, LANES), jnp.float32),
             pltpu.VMEM((blocks * height, 4 * LANES), jnp.float32),
             pltpu.VMEM((STEPS, rows, NY), jnp.float32),

time: 46.4 us -> 42 us (0.905)
  Pallas kernels: 43.2 us -> 38.8 us
    pallas_call x1, Pallas kernels: 43.2 us -> 38.8 us  [body(): pl.pallas_call(functools.partial(kernel, freqs, tiles), out_shape=(jax.Sh...]
where the time goes in v3:
time: 42 us; the launch traced here: 41.9 us
  Pallas kernels  38.8 us (92%)
  local copies, waits for them, and re-layouts  2.45 us (6%)
  between operations  0.65 us (2%)
    pallas_call x1, Pallas kernels, body(): pl.pallas_call(functools.partial(kernel, freqs, tiles), out_shape=(jax.Sh...  38.8 us
    unnamed x4, local copies, waits for them, and re-layouts  2.45 us

profile of v3, /device:TPU:0, one launch (start us, length us, event | category | flops | bytes accessed | tf_op | source)
XLA Modules:
  0.0 41.9 jit_solution(3479683292176797123)
XLA Ops:
  0.6 38.8 %shard_map.68 = (f32[2,1,2,24,1024]{4,3,2,1,0:T(8,128)}, f32[4,24,256]{2,1,0:T(8,128)}) custom-call(f32[4,24,256]{2,1,0:T(8,128)} %velocity.1, s32[1,4096]{1,0:T(1,128)} %bitcast.3, f32[2,1,4096]{2,1,0:T(1,128)} %src_wave_in.1, s32[1,16384]{1,0:T(1,128)} %bitcast.2, f32[2,1,16384]{2,1,0:T(1,128)} %rec_data_in.1), custom_call_target="tpu_custom_call" | custom-call | tf_op jit(solution)/shard_map/pallas_call | solution.py:481
  39.4 0.0 copy-start
  39.4 1.8 %copy.9 = f32[2,1,2,24,1024]{4,3,2,1,0:T(8,128)} copy(f32[2,1,2,24,1024]{4,3,2,1,0:T(8,128)} %get-tuple-element.4) | data formatting | bytes 786432
  41.2 0.0 copy-done
  41.2 0.6 %copy.10 = f32[4,24,256]{2,1,0:T(8,128)} copy(f32[4,24,256]{2,1,0:T(8,128)S(1)} %copy-done) | data formatting | bytes 196608
Async XLA Ops:
  39.4 1.8 %copy-start = (f32[4,24,256]{2,1,0:T(8,128)S(1)}, f32[4,24,256]{2,1,0:T(8,128)}, u32[]{:S(2)}) copy-start(f32[4,24,256]{2,1,0:T(8,128)} %get-tuple-element.5) | copy-start | bytes 294916

commit v4 on v3

--- a/solution.py
+++ b/solution.py
@@ -397,7 +397,7 @@
                         terms[k, plane, b, pl.ds(top, SUBLANES), :] = new
                 return carry
 
-            lax.fori_loop(0, 4, advance, 0)
+            lax.fori_loop(0, 4, advance, 0, unroll=2)
 
         def combine(b, carry):
             for s in strips(margin):
@@ -423,7 +423,7 @@
                     )
             return carry
 
-        lax.fori_loop(0, blocks, combine, 0)
+        lax.fori_loop(0, blocks, combine, 0, unroll=2)
         if z == STEPS - 2:
             finish_images(0, STEPS - 1)
         elif z == STEPS - 1:

time: 42 us -> 41 us (0.976)
  Pallas kernels: 38.8 us -> 37.7 us
    pallas_call x1, Pallas kernels: 38.8 us -> 37.7 us  [body(): pl.pallas_call(functools.partial(kernel, freqs, tiles), out_shape=(jax.Sh...]
where the time goes in v4:
time: 41 us; the launch traced here: 40.8 us
  Pallas kernels  37.7 us (92%)
  local copies, waits for them, and re-layouts  2.45 us (6%)
  between operations  0.65 us (2%)
    pallas_call x1, Pallas kernels, body(): pl.pallas_call(functools.partial(kernel, freqs, tiles), out_shape=(jax.Sh...  37.7 us
    unnamed x4, local copies, waits for them, and re-layouts  2.45 us

profile of v4, /device:TPU:0, one launch (start us, length us, event | category | flops | bytes accessed | tf_op | source)
XLA Modules:
  0.0 40.8 jit_solution(9070989590771627476)
XLA Ops:
  0.6 37.7 %shard_map.68 = (f32[2,1,2,24,1024]{4,3,2,1,0:T(8,128)}, f32[4,24,256]{2,1,0:T(8,128)}) custom-call(f32[4,24,256]{2,1,0:T(8,128)} %velocity.1, s32[1,4096]{1,0:T(1,128)} %bitcast.3, f32[2,1,4096]{2,1,0:T(1,128)} %src_wave_in.1, s32[1,16384]{1,0:T(1,128)} %bitcast.2, f32[2,1,16384]{2,1,0:T(1,128)} %rec_data_in.1), custom_call_target="tpu_custom_call" | custom-call | tf_op jit(solution)/shard_map/pallas_call | solution.py:481
  38.4 0.0 copy-start
  38.4 1.8 %copy.9 = f32[2,1,2,24,1024]{4,3,2,1,0:T(8,128)} copy(f32[2,1,2,24,1024]{4,3,2,1,0:T(8,128)} %get-tuple-element.4) | data formatting | bytes 786432
  40.2 0.0 copy-done
  40.2 0.6 %copy.10 = f32[4,24,256]{2,1,0:T(8,128)} copy(f32[4,24,256]{2,1,0:T(8,128)S(1)} %copy-done) | data formatting | bytes 196608
Async XLA Ops:
  38.4 1.8 %copy-start = (f32[4,24,256]{2,1,0:T(8,128)S(1)}, f32[4,24,256]{2,1,0:T(8,128)}, u32[]{:S(2)}) copy-start(f32[4,24,256]{2,1,0:T(8,128)} %get-tuple-element.5) | copy-start | bytes 294916
